TPU v7x, 32 devices: a whole 2x2x4 slice. The times are simulated.
32 devices in a mesh: groups: 2 (over x), blk: 16 (over z, y, core).
Axes of the slice: x: 2, y: 2, z: 4, core: 2. Of those that a mesh axis runs over, the one named last changes fastest.
Arguments:
- walkers: bfloat16 [64, 65536], P(('groups', 'blk')), parts along dimension 0, may hold values from -6 to 6
- intersection_inv: bfloat16 [64, 4096], P(('groups', 'blk')), parts along dimension 0, may hold values from -0.75 to 0.75
- new_slot: int32 [64], P(('groups', 'blk')), parts along dimension 0, may hold values from 0 to 31, as said below
- cholesky: bfloat16 [2048, 64, 10240], P(('groups', 'blk')), parts along dimension 0, may hold values from -0.0234375 to 0.0234375
Outputs:
- moved_walkers: bfloat16 [64, 65536], P(('groups', 'blk')), parts along dimension 0
- moved_intersection_inv: bfloat16 [64, 4096], P(('groups', 'blk')), parts along dimension 0
- force_bias: float32 [64, 10240], P(('groups', 'blk')), parts along dimension 0
There are 2 independent parts, one for each index of `groups`. A program takes and returns all parts, laid end to end along the dimension named above; each array names one. Nothing has to cross between parts.
Inputs may be any that keep to these rules, and one draw needn't show every extreme that they name: new_slot is a permutation; the new owner of walker w is new_slot[w] // 2; the 2 walkers of one device go to 2 different owners, and new_slot[w] % 2 == w % 2.
All inputs are finite; a program needn't handle non-finite values.
Results may differ from a plain program's by a relative error of at most 0.0028.
Values may be sent and summed in bfloat16 or wider, within the bound.
A program may use at most 128 MiB of HBM per device.

v0:
```python
import jax
import jax.numpy as jnp
from jax import lax
from jax.sharding import PartitionSpec as P


def local(walkers, intersection_inv, new_slot, cholesky):
    cycle_size = lax.axis_size("blk")
    my_index = lax.axis_index("blk")
    walk_dev = walkers.shape[0]
    walk_total = walk_dev * cycle_size
    orbit_local = cholesky.shape[0]
    occupied = cholesky.shape[1]
    chol_flat = cholesky.reshape(orbit_local * occupied, cholesky.shape[2])
    all_slots = lax.all_gather(new_slot, "blk", axis=0, tiled=True)
    anchor = (
        jnp.zeros((walk_total,), jnp.int32)
        .at[all_slots]
        .set(jnp.arange(walk_total, dtype=jnp.int32))
    )
    local_orbit = lax.all_to_all(walkers, "blk", split_axis=1, concat_axis=0, tiled=True)
    all_inverse = lax.all_gather(intersection_inv, "blk", axis=0, tiled=True)
    perm_orbit = local_orbit[anchor]
    perm_inverse = all_inverse[anchor]
    greens = jnp.einsum(
        "wpj,wij->wpi",
        perm_orbit.reshape(walk_total, orbit_local, occupied),
        perm_inverse.reshape(walk_total, occupied, occupied),
        preferred_element_type=jnp.float32,
    ).astype(jnp.bfloat16)
    green_orbit = greens.reshape(walk_total, orbit_local * occupied)
    moved_walk = lax.all_to_all(perm_orbit, "blk", split_axis=0, concat_axis=1, tiled=True)
    moved_inverse = lax.dynamic_slice_in_dim(perm_inverse, my_index * walk_dev, walk_dev, 0)
    force_bias = lax.psum_scatter(
        jnp.dot(green_orbit, chol_flat, preferred_element_type=jnp.float32),
        "blk",
        scatter_dimension=0,
        tiled=True,
    )
    return (moved_walk, moved_inverse, force_bias)


def solution(mesh):
    placed = (
        P(("groups", "blk"), None),
        P(("groups", "blk"), None),
        P(("groups", "blk")),
        P(("groups", "blk"), None, None),
    )
    return jax.shard_map(
        local,
        mesh=mesh,
        in_specs=placed,
        out_specs=(
            P(("groups", "blk"), None),
            P(("groups", "blk"), None),
            P(("groups", "blk"), None),
        ),
        check_vma=False,
    )
```

profile of v0, /device:TPU:0, one launch (start us, length us, event | category | flops | bytes accessed | tf_op | source)
XLA Modules:
  0.0 186.4 jit_solution(3166553028669388083)
XLA Ops:
  7.2 7.4 %all-to-all-start = ((bf16[2,16,4096]{2,0,1:T(2,128)(2,1)}), bf16[2,16,4096]{2,0,1:T(2,128)(2,1)S(1)}, u32[]{:S(2)}, u32[]{:S(2)}) async-start(bf16[2,16,4096]{2,0,1:T(2,128)(2,1)} %bitcast.16), calls=%async_computation | async-start | bytes 524288 | tf_op jit(solution)/shard_map/all_to_all | solution.py:21
  14.6 0.0 all-reduce.4.cloned.1.call-start
  14.6 1.3 fusion.2
  16.6 0.9 dynamic-update-slice
  17.5 12.4 %all-reduce = s32[32]{0:T(128)S(1)} all-reduce(s32[32]{0:T(128)S(1)} %dynamic-update-slice), channel_id=1, replica_groups=mesh['groups'=2,'blk'=16] {'blk'}, use_global_device_ids=true, to_apply=%add | all-reduce | flops 32 | bytes 256
  29.9 18.9 %all-gather = bf16[16,2,4096]{2,1,0:T(2,128)(2,1)S(1)} all-gather(bf16[1,2,4096]{2,1,0:T(2,128)(2,1)} %bitcast.17), channel_id=1, replica_groups=mesh['groups'=2,'blk'=16] {'blk'}, dimensions={0}, use_global_device_ids=true | all-gather | bytes 278528 | tf_op jit(solution)/shard_map/all_gather | solution.py:22
  48.8 0.1 reshape.53
  48.9 0.7 scatter_custom_fusion
  49.6 0.7 gather_fusion.1
  50.3 0.5 reshape.21
  50.8 0.0 all-to-all-done
  50.9 0.1 all_to_all.31
  51.0 0.7 gather_fusion
  51.7 0.5 reshape.20
  52.2 0.4 fusion.3
  52.6 30.0 %convolution_bitcast_fusion = f32[32,10240]{1,0:T(8,128)} fusion(bf16[64,64,10240]{2,1,0:T(8,128)(2,1)} %param.7, bf16[32,64,64]{2,1,0:T(8,128)(2,1)S(1)} %fusion.3), kind=kOutput, calls=%fused_computation.3 | convolution fusion | flops 2684354560 | bytes 85458944 | tf_op jit(solution)/shard_map/dot_general | solution.py:35
  82.6 0.0 all-reduce.4.cloned.1.call-update
  82.7 0.9 all_to_all.32
  83.5 3.5 %all-to-all-start.1 = ((bf16[16,2,4096]{2,1,0:T(2,128)(2,1)}), bf16[16,2,4096]{2,1,0:T(2,128)(2,1)S(1)}, u32[]{:S(2)}, u32[]{:S(2)}) async-start(bf16[16,2,4096]{2,1,0:T(2,128)(2,1)} %all_to_all.32), calls=%async_computation.1 | async-start | bytes 524288 | tf_op jit(solution)/shard_map/all_to_all | solution.py:32
  87.7 0.6 constant_dynamic-slice_fusion.1
  88.4 11.0 %all-to-all-done.1 = bf16[16,2,4096]{2,1,0:T(2,128)(2,1)S(1)} async-done(((bf16[16,2,4096]{2,1,0:T(2,128)(2,1)}), bf16[16,2,4096]{2,1,0:T(2,128)(2,1)S(1)}, u32[]{:S(2)}, u32[]{:S(2)}) %all-to-all-start.1) | async-done | bytes 262176 | tf_op jit(solution)/shard_map/all_to_all | solution.py:32
  99.4 77.8 %all-reduce.4.cloned.1.call-done = f32[32,10240]{1,0:T(8,128)} async-done(((f32[32,10240]{1,0:T(8,128)}), f32[32,10240]{1,0:T(8,128)}) %all-reduce.4.cloned.1.call-update) | async-done | bytes 1310736
  177.2 1.6 constant_dynamic-slice_fusion
  178.9 0.7 copy.17
  (5 shorter events, 0.0 us)
Async XLA Ops:
  7.2 43.7 %all-to-all-start = ((bf16[2,16,4096]{2,0,1:T(2,128)(2,1)}), bf16[2,16,4096]{2,0,1:T(2,128)(2,1)S(1)}, u32[]{:S(2)}, u32[]{:S(2)}) async-start(bf16[2,16,4096]{2,0,1:T(2,128)(2,1)} %bitcast.16), calls=%async_computation | async-start | bytes 524288 | tf_op jit(solution)/shard_map/all_to_all | solution.py:21
  14.6 162.7 %all-reduce.4.cloned.1.call-start = ((), (), s32[]{:S(2)}) async-start(), calls=%async_computation.2 | async-start | bytes 2621440
  83.5 15.9 %all-to-all-start.1 = ((bf16[16,2,4096]{2,1,0:T(2,128)(2,1)}), bf16[16,2,4096]{2,1,0:T(2,128)(2,1)S(1)}, u32[]{:S(2)}, u32[]{:S(2)}) async-start(bf16[16,2,4096]{2,1,0:T(2,128)(2,1)} %all_to_all.32), calls=%async_computation.1 | async-start | bytes 524288 | tf_op jit(solution)/shard_map/all_to_all | solution.py:32
Sparse Core Ops, SparseCore 0:
  82.8 94.4 all-reduce.3
where the time goes:
time: 187 us; the launch traced here: 186 us
  waiting for transfers between devices  88.9 us (48%)
  blocking collectives  31.3 us (17%)
  matrix products  30.4 us (16%)
  between operations  15.5 us (8%)
  starting transfers between devices  11 us (6%)
  local copies, waits for them, and re-layouts  9.4 us (5%)
    unnamed x2, waiting for transfers between devices  77.8 us
    dot_general x1, matrix products, local(): jnp.dot(green_orbit, chol_flat, preferred_element_type=jnp.float32)  30 us
    all_gather x1, blocking collectives, local(): all_inverse = lax.all_gather(intersection_inv, 'blk', axis=0, tiled=True)  18.9 us
    unnamed x1, blocking collectives  12.4 us
    all_to_all x1, waiting for transfers between devices, local(): lax.all_to_all(perm_orbit, 'blk', split_axis=0, concat_axis=1, tiled=True)  11 us
    all_to_all x1, starting transfers between devices, local(): lax.all_to_all(walkers, 'blk', split_axis=1, concat_axis=0, tiled=True)  7.4 us
    unnamed x5, local copies, waits for them, and re-layouts  4.62 us
  transfers between devices with their start and end apart: 3, of which 2 were waited for; matrix products, arithmetic and copies ran while one was open for 3% of the time, Pallas kernels for 0%

commit v1 on v0

v1 whole, which is shorter than its diff:
```python
import functools

import jax
import jax.numpy as jnp
from jax import lax
from jax.experimental import pallas as pl
from jax.experimental.pallas import tpu as pltpu
from jax.sharding import PartitionSpec as P

MESH = pl.DeviceIdType.MESH
LANES = 128
MIB = 2**20


def kernel(
    n, wd, rows, tail, batches, per_batch, slots, anchor_rows,
    wk_ref, iv_ref, bd_ref, contrib_ref, chol_ref,
    moved_ref, force_ref,
    ring, gsend, grecv, wsend, wrecv, msend, arecv, anchor_v, anchor_s,
    gflat, green, ftmp, fsend, frecv,
    ring_sem, local_sem, send_sem, recv_sem,
):
    me = lax.axis_index("blk")
    wt = n * wd
    cols = ring.shape[2]
    tiles = cols // LANES
    span = tiles * per_batch
    chunks = batches * per_batch
    blk = wd * rows

    def fetch(c, k):
        return pltpu.make_async_copy(
            chol_ref.at[:, pl.ds(pl.multiple_of(c * cols, cols), cols)],
            ring.at[k],
            ring_sem.at[k],
        )

    def peers(body):
        def one(i, carry):
            body(lax.rem(me + i, n))
            return carry

        lax.fori_loop(1, n, one, 0)

    def push(src_of, dst, k):
        def one(to):
            pltpu.make_async_remote_copy(
                src_ref=src_of(to), dst_ref=dst,
                send_sem=send_sem.at[k], recv_sem=recv_sem.at[k],
                device_id={"blk": to}, device_id_type=MESH,
            ).start()

        peers(one)

    def drain(buf, sem):
        part = buf.at[pl.ds(0, n - 1)]
        pltpu.make_async_copy(part, part, sem).wait()

    barrier = pltpu.get_barrier_semaphore()
    peers(
        lambda to: pl.semaphore_signal(
            barrier, inc=1, device_id={"blk": to}, device_id_type=MESH
        )
    )

    for c in range(slots):
        fetch(c, c).start()

    group = min(n, 16)

    def make(g, carry):
        at = pl.multiple_of(g * group * rows, group * rows)
        for w in range(wd):
            x = lax.dot_general(
                wk_ref[w, pl.ds(at, group * rows), :], bd_ref[w],
                (((1,), (1,)), ((), ())), preferred_element_type=jnp.float32,
            ).astype(jnp.bfloat16)
            for d in range(group):
                gsend[g * group + d, w * rows:(w + 1) * rows, :] = x[d * rows:(d + 1) * rows]
        return carry

    lax.fori_loop(0, n // group, make, 0)

    pl.semaphore_wait(barrier, n - 1)
    push(lambda to: contrib_ref, arecv.at[me], 0)
    push(lambda to: gsend.at[to], grecv.at[me], 1)

    def lay(d, carry):
        at = pl.multiple_of(d * rows, rows)
        for w in range(wd):
            wsend[d, w * rows:(w + 1) * rows, :] = wk_ref[w, pl.ds(at, rows), :]
        wsend[d, blk:blk + tail, :] = iv_ref[d]
        return carry

    lax.fori_loop(0, n, lay, 0)
    arecv[me] = contrib_ref[...]
    grecv[me] = gsend[me]
    wrecv[me] = wsend[me]

    drain(arecv, recv_sem.at[0])

    def add(d, total):
        return total + arecv[d]

    anchor_v[...] = lax.fori_loop(0, n, add, jnp.zeros((anchor_rows, LANES), jnp.int32))
    to_scalar = pltpu.make_async_copy(anchor_v, anchor_s, local_sem)
    to_scalar.start()
    to_scalar.wait()

    drain(grecv, recv_sem.at[1])

    def source(s):
        return anchor_s[s // LANES, s % LANES] // wd

    def permute(d, carry):
        for w in range(wd):
            s = d * wd + w
            at = pl.multiple_of(s * rows, rows)
            gflat[pl.ds(at, rows), :] = grecv[
                source(s), w * rows:(w + 1) * rows, :
            ].astype(jnp.float32)
        return carry

    lax.fori_loop(0, n, permute, 0)
    for r in range(green.shape[1] // LANES):
        green[:, r * LANES:(r + 1) * LANES] = gflat[
            pl.ds(r, wt, stride=rows), :
        ].astype(jnp.bfloat16)

    def move(d, carry):
        for w in range(wd):
            msend[d, w * rows:(w + 1) * rows, :] = wrecv[
                source(d * wd + w), w * rows:(w + 1) * rows, :
            ]
        row = lax.broadcasted_iota(jnp.int32, (tail, LANES), 0)
        piece = jnp.zeros((tail, LANES), jnp.float32)
        for w in range(wd):
            got = wrecv[source(d * wd + w), blk:blk + tail, :].astype(jnp.float32)
            piece = jnp.where(row // (tail // wd) == w, got, piece)
        msend[d, blk:blk + tail, :] = piece.astype(jnp.bfloat16)
        return carry

    def step(c, carry):
        k = lax.rem(c, slots)
        b = c // per_batch
        q = lax.rem(c, per_batch)
        fetch(c, k).wait()
        acc = jnp.dot(green[...], ring[k], preferred_element_type=jnp.float32)

        @pl.when(c + slots < chunks)
        def _():
            fetch(c + slots, k).start()

        for j in range(tiles):
            ftmp[pl.ds(q * tiles + j, wt, stride=span), :] = acc[:, j * LANES:(j + 1) * LANES]

        @pl.when(c == 0)
        def _():
            push(lambda to: wsend.at[to], wrecv.at[me], 2)

        @pl.when(c == min(chunks - 1, 6))
        def _():
            drain(wrecv, recv_sem.at[2])
            lax.fori_loop(0, n, move, 0)
            push(lambda to: msend.at[to], moved_ref.at[me], 3)
            moved_ref[me] = msend[me]

        @pl.when(q == per_batch - 1)
        def _():
            size = wd * span

            def cast(d, carry):
                at = pl.multiple_of(d * size, size)
                fsend[b, d] = ftmp[pl.ds(at, size), :].astype(jnp.bfloat16)
                return carry

            lax.fori_loop(0, n, cast, 0)
            force_ref[b] = ftmp[pl.ds(pl.multiple_of(me * size, size), size), :]
            push(lambda to: fsend.at[b, to], frecv.at[b, me], 4 + b)

        return carry

    lax.fori_loop(0, chunks, step, 0)

    def finish(b, carry):
        drain(frecv.at[b], recv_sem.at[4 + b])

        def plus(i, total):
            return total + frecv[b, lax.rem(me + i, n)].astype(jnp.float32)

        force_ref[b] = lax.fori_loop(1, n, plus, force_ref[b])
        return carry

    lax.fori_loop(0, batches, finish, 0)
    drain(moved_ref, recv_sem.at[3])
    drain(arecv, send_sem.at[0])
    drain(gsend, send_sem.at[1])
    drain(wsend, send_sem.at[2])
    drain(msend, send_sem.at[3])

    def sent(b, carry):
        drain(fsend.at[b], send_sem.at[4 + b])
        return carry

    lax.fori_loop(0, batches, sent, 0)


def local(walkers, intersection_inv, new_slot, cholesky):
    n = lax.axis_size("blk")
    me = lax.axis_index("blk")
    wd = walkers.shape[0]
    wt = n * wd
    orbitals, occ, ncol = cholesky.shape
    depth = orbitals * occ
    real = depth // LANES
    rows = -(-real // 16) * 16
    chol = cholesky.reshape(depth, ncol)

    wk = walkers.reshape(wd, n * real, LANES)
    if rows != real:
        wk = jnp.pad(
            wk.reshape(wd, n, real, LANES), ((0, 0), (0, 0), (0, rows - real), (0, 0))
        ).reshape(wd, n * rows, LANES)
    inv = intersection_inv.reshape(wd, occ, occ)
    pack = LANES // occ
    eye = jnp.eye(pack, dtype=jnp.bfloat16)
    bd = (eye[None, :, None, :, None] * inv[:, None, :, None, :]).reshape(wd, LANES, LANES)
    share = occ * occ // n
    part = max(16 // wd, -(-share // LANES))
    tail = wd * part
    iv = jnp.pad(
        intersection_inv.reshape(wd, n, share).transpose(1, 0, 2),
        ((0, 0), (0, 0), (0, part * LANES - share)),
    ).reshape(n, tail, LANES)
    anchor_rows = 8 * -(-wt // (8 * LANES))
    place = lax.broadcasted_iota(jnp.int32, (anchor_rows, LANES), 0) * LANES
    place = place + lax.broadcasted_iota(jnp.int32, (anchor_rows, LANES), 1)
    contrib = jnp.zeros((anchor_rows, LANES), jnp.int32)
    for w in range(wd):
        contrib = jnp.where(place == new_slot[w], me * wd + w, contrib)

    cols = 512
    per_batch = 4 if ncol % 2048 == 0 else 2
    chunks = ncol // cols
    batches = chunks // per_batch
    span = per_batch * cols // LANES
    bf, f32 = jnp.bfloat16, jnp.float32
    blk = wd * rows
    bufs = [
        ((n, blk, LANES), bf),
        ((n, blk, LANES), bf),
        ((n, blk + tail, LANES), bf),
        ((n, blk + tail, LANES), bf),
        ((n, blk + tail, LANES), bf),
        ((n, anchor_rows, LANES), jnp.int32),
        ((anchor_rows, LANES), jnp.int32),
    ]
    more = [
        ((wt * rows, LANES), f32),
        ((wt, depth), bf),
        ((wt * span, LANES), f32),
        ((batches, n, wd * span, LANES), bf),
        ((batches, n, wd * span, LANES), bf),
    ]

    def size(shape, dtype):
        total = jnp.dtype(dtype).itemsize
        for d in shape:
            total *= d
        return total

    used = sum(size(*b) for b in bufs + more)
    used += 2 * size((n, blk + tail, LANES), bf) + size((wd, ncol), f32)
    slots = min(chunks, (56 * MIB - used) // size((depth, cols), bf))

    vmem = pl.BlockSpec(memory_space=pltpu.VMEM)
    moved, force = pl.pallas_call(
        functools.partial(
            kernel, n, wd, rows, tail, batches, per_batch, slots, anchor_rows
        ),
        out_shape=(
            jax.ShapeDtypeStruct((n, blk + tail, LANES), bf),
            jax.ShapeDtypeStruct((batches, wd * span, LANES), f32),
        ),
        in_specs=[vmem, vmem, vmem, vmem, pl.BlockSpec(memory_space=pl.ANY)],
        out_specs=(vmem, vmem),
        scratch_shapes=[
            pltpu.VMEM((slots, depth, cols), bf),
            *[pltpu.VMEM(*b) for b in bufs],
            pltpu.SMEM((anchor_rows, LANES), jnp.int32),
            *[pltpu.VMEM(*b) for b in more],
            pltpu.SemaphoreType.DMA((slots,)),
            pltpu.SemaphoreType.DMA,
            pltpu.SemaphoreType.DMA((4 + batches,)),
            pltpu.SemaphoreType.DMA((4 + batches,)),
        ],
        compiler_params=pltpu.CompilerParams(
            collective_id=0, has_side_effects=True, vmem_limit_bytes=60 * MIB
        ),
        cost_estimate=pl.CostEstimate(
            flops=2 * wt * depth * ncol, bytes_accessed=2 * depth * ncol, transcendentals=0
        ),
    )(wk, iv, bd, contrib, chol)

    moved_walk = (
        moved[:, :blk].reshape(n, wd, rows, LANES)[:, :, :real]
        .transpose(1, 0, 2, 3).reshape(wd, n * depth)
    )
    moved_inverse = (
        moved[:, blk:].reshape(n, wd, part * LANES)[:, :, :share]
        .transpose(1, 0, 2).reshape(wd, occ * occ)
    )
    force_bias = (
        force.reshape(batches, wd, span * LANES).transpose(1, 0, 2).reshape(wd, ncol)
    )
    return (moved_walk, moved_inverse, force_bias)


def solution(mesh):
    placed = (
        P(("groups", "blk"), None),
        P(("groups", "blk"), None),
        P(("groups", "blk")),
        P(("groups", "blk"), None, None),
    )
    return jax.shard_map(
        local,
        mesh=mesh,
        in_specs=placed,
        out_specs=(
            P(("groups", "blk"), None),
            P(("groups", "blk"), None),
            P(("groups", "blk"), None),
        ),
        check_vma=False,
    )
```

time: 187 us -> 62.4 us (0.33)
  waiting for transfers between devices: 88.9 us -> 0 us
  Pallas kernels: 0 us -> 48 us
  blocking collectives: 31.3 us -> 0 us
  matrix products: 30.4 us -> 0 us
  between operations: 15.5 us -> 0.71 us
  starting transfers between devices: 11 us -> 0 us
  other arithmetic: 0.01 us -> 2.6 us
    unnamed x2 -> x0, waiting for transfers between devices: 77.8 us -> none
    pallas_call x0 -> x1, Pallas kernels: none -> 48 us  [local(): pl.pallas_call(functools.partial(kernel, n, wd, rows, tail, batches, per_...]
    dot_general x2 -> x0, matrix products: 30.4 us -> none  [the longest x1 30 us: local(): jnp.dot(green_orbit, chol_flat, preferred_element_type=jnp.float32)]
    all_gather x1 -> x0, blocking collectives: 18.9 us -> none  [local(): all_inverse = lax.all_gather(intersection_inv, 'blk', axis=0, tiled=True)]
    unnamed x1 -> x0, blocking collectives: 12.4 us -> none
    all_to_all x2 -> x0, waiting for transfers between devices: 11 us -> none  [the longest x1 11 us: local(): lax.all_to_all(perm_orbit, 'blk', split_axis=0, concat_axis=1, tiled=True)]
    all_to_all x2 -> x0, starting transfers between devices: 10.9 us -> none  [the longest x1 7.4 us: local(): lax.all_to_all(walkers, 'blk', split_axis=1, concat_axis=0, tiled=True)]
    slice x0 -> x4, local copies, waits for them, and re-layouts: none -> 3.75 us  [the longest x2 1.47 us: local(): moved[:, blk:].reshape(n, wd, part * LANES)[:, :, :share].transpose(1, 0, 2)]
  transfers between devices with their start and end apart: 3 -> 0, of which waited for: 2 -> 0; matrix products, arithmetic and copies ran while one was open for 3% -> 0% of each run, Pallas kernels for 0% -> 0%
where the time goes in v1:
time: 62.4 us; the launch traced here: 62 us
  Pallas kernels  48 us (77%)
  local copies, waits for them, and re-layouts  10.8 us (17%)
  other arithmetic  2.6 us (4%)
  between operations  0.71 us (1%)
    pallas_call x1, Pallas kernels, local(): pl.pallas_call(functools.partial(kernel, n, wd, rows, tail, batches, per_...  48 us
    unnamed x3, local copies, waits for them, and re-layouts  3.36 us
    select_n x1, other arithmetic, local(): contrib = jnp.where(place == new_slot[w], me * wd + w, contrib)  1.96 us
    slice x2, local copies, waits for them, and re-layouts, local(): moved[:, blk:].reshape(n, wd, part * LANES)[:, :, :share].transpose(1, 0, 2)  1.47 us
    slice x1, local copies, waits for them, and re-layouts, local(): contrib = jnp.where(place == new_slot[w], me * wd + w, contrib)  1.31 us

profile of v1, /device:TPU:0, one launch (start us, length us, event | category | flops | bytes accessed | tf_op | source)
XLA Modules:
  0.0 62.0 jit_solution(17637780556169673127)
XLA Ops:
  0.7 1.3 %fusion.2 = (s32[1]{0:T(128)}, s32[1]{0:T(128)}) fusion(s32[2]{0:T(128)} %param.6), kind=kLoop, calls=%fused_computation.10 | loop fusion | bytes 16 | tf_op jit(solution)/shard_map/slice | solution.py:240
  2.0 2.0 %select_select_fusion.contrib_ref = s32[8,128]{1,0:T(8,128)} fusion(s32[]{:T(128)S(6)} %mul.44, s32[]{:T(128)} %bitcast.3, s32[]{:T(128)S(6)} %add.11, s32[]{:T(128)} %bitcast.2, s32[8]{0:T(128)S(1)} %iota_multiply_fusion), kind=kLoop, calls=%fused_computation.4 | loop fusion | flops 5120 | bytes 4144 | tf_op jit(solution)/shard_map/jit(_where)/select_n | solution.py:240
  3.9 0.8 %mul.38 = bf16[2,64,64]{2,1,0:T(8,128)(2,1)S(1)} reshape(bf16[2,4096]{1,0:T(2,128)(2,1)} %param.5) | data formatting | bytes 32768 | tf_op jit(solution)/shard_map/mul | solution.py:227
  4.7 0.1 mul.35
  4.8 0.1 mul.36
  4.9 0.8 %pad.4 = bf16[16,2,1024]{2,1,0:T(2,128)(2,1)S(1)} pad(bf16[16,2,256]{2,1,0:T(2,128)(2,1)} %bitcast.33, bf16[]{:T(256)} %constant.6.clone.1), padding=0_0x0_0x0_768 | pad | bytes 81922 | tf_op jit(solution)/shard_map/jit(_pad)/pad | solution.py:231
  5.7 0.7 %reshape.50.iv_ref = bf16[16,16,128]{2,1,0:T(8,128)(2,1)} reshape(bf16[16,2,1024]{2,1,0:T(2,128)(2,1)S(1)} %pad.4) | data formatting | bytes 131072 | tf_op jit(solution)/shard_map/reshape | solution.py:234
  6.4 0.1 mul.39
  6.5 0.1 mul.40
  6.6 0.6 %broadcast_multiply_fusion.bd_ref = bf16[2,128,128]{2,1,0:T(8,128)(2,1)} fusion(bf16[2,128,128]{2,1,0:T(8,128)(2,1)S(1)} %mul.40, bf16[128,128]{1,0:T(8,128)(2,1)S(1)} %mul.36), kind=kLoop, calls=%fused_computation.3 | loop fusion | flops 32768 | bytes 163840 | tf_op jit(solution)/shard_map/mul | solution.py:227
  7.2 1.7 %copy.22 = bf16[1,2,512,128]{3,2,1,0:T(8,128)(2,1)} copy(bf16[1,2,512,128]{3,1,2,0:T(2,128)(2,1)} %bitcast.30) | data formatting | bytes 524288
  8.9 48.0 %shard_map.67 = (bf16[16,80,128]{2,1,0:T(8,128)(2,1)}, f32[5,32,128]{2,1,0:T(8,128)}) custom-call(bf16[2,512,128]{2,1,0:T(8,128)(2,1)} %bitcast.26, bf16[16,16,128]{2,1,0:T(8,128)(2,1)} %reshape.50.iv_ref, bf16[2,128,128]{2,1,0:T(8,128)(2,1)} %broadcast_multiply_fusion.bd_ref, s32[8,128]{1,0:T(8,128)} %select_select_fusion.contrib_ref, ...), custom_call_target="tpu_custom_call" | custom-call | flops 2684354560 | bytes 83886080 | tf_op jit(solution)/shard_map/pallas_call | solution.py:277
  56.9 0.9 %reshape.56 = f32[5,2,2048]{2,1,0:T(2,128)S(1)} reshape(f32[5,32,128]{2,1,0:T(8,128)} %get-tuple-element.6) | data formatting | bytes 163840 | tf_op jit(solution)/shard_map/reshape | solution.py:314
  57.8 0.1 copy.23
  57.9 0.7 %copy.17 = f32[1,2,5,2048]{3,1,2,0:T(2,128)} copy(f32[1,2,5,2048]{3,2,1,0:T(8,128)S(1)} %bitcast.29) | data formatting | bytes 163840
  58.6 0.8 %slice.18 = bf16[16,16,128]{2,1,0:T(8,128)(2,1)S(1)} slice(bf16[16,80,128]{2,1,0:T(8,128)(2,1)} %get-tuple-element.5), slice={[0:16], [64:80], [0:128]} | slice | bytes 131072 | tf_op jit(solution)/shard_map/slice | solution.py:310
  59.4 1.0 %slice.17 = bf16[16,64,128]{2,1,0:T(8,128)(2,1)S(1)} slice(bf16[16,80,128]{2,1,0:T(8,128)(2,1)} %get-tuple-element.5), slice={[0:16], [0:64], [0:128]} | slice | bytes 524288 | tf_op jit(solution)/shard_map/slice | solution.py:306
  60.4 1.0 %copy.21 = bf16[1,2,512,128]{3,1,2,0:T(2,128)(2,1)} copy(bf16[1,2,512,128]{3,2,1,0:T(8,128)(2,1)S(1)} %bitcast.28) | data formatting | bytes 524288
  61.4 0.6 %slice.20 = bf16[16,2,256]{2,1,0:T(2,128)(2,1)} slice(bf16[16,2,1024]{2,1,0:T(2,128)(2,1)S(1)} %reshape.54), slice={[0:16], [0:2], [0:256]} | slice | bytes 32768 | tf_op jit(solution)/shard_map/slice | solution.py:310
  (4 shorter events, 0.0 us)

commit v2 on v1

v2 whole, which is shorter than its diff:
```python
import functools

import jax
import jax.numpy as jnp
from jax import lax
from jax.experimental import pallas as pl
from jax.experimental.pallas import tpu as pltpu
from jax.sharding import PartitionSpec as P

MESH = pl.DeviceIdType.MESH
LANES = 128
MIB = 2**20


def kernel(
    n, wd, occ, rows, tail, batches, per_batch, slots, anchor_rows,
    wk_ref, iv_ref, slot_ref, chol_ref,
    walk_ref, piece_ref, force_ref,
    ring, gsend, grecv, wsend, wrecv, msend, mrecv, contrib, arecv, anchor_v,
    anchor_s, ivf, bdf, gflat, green, ftmp, xrecv, fsend, frecv, own,
    ring_sem, local_sem, send_sem, recv_sem,
):
    me = lax.axis_index("blk")
    wt = n * wd
    cols = ring.shape[2]
    tiles = cols // LANES
    span = tiles * per_batch
    chunks = batches * per_batch
    blk = wd * rows
    chips = n // 2
    chip, core = me // 2, lax.rem(me, 2)
    size = wd * span
    half = chips * size

    def fetch(c, k):
        return pltpu.make_async_copy(
            chol_ref.at[:, pl.ds(pl.multiple_of(c * cols, cols), cols)],
            ring.at[k],
            ring_sem.at[k],
        )

    def peers(body):
        def one(i, carry):
            body(lax.rem(me + i, n))
            return carry

        lax.fori_loop(1, n, one, 0)

    def push(src_of, dst, k):
        def one(to):
            pltpu.make_async_remote_copy(
                src_ref=src_of(to), dst_ref=dst,
                send_sem=send_sem.at[k], recv_sem=recv_sem.at[k],
                device_id={"blk": to}, device_id_type=MESH,
            ).start()

        peers(one)

    def drain(buf, sem, count):
        part = buf.at[pl.ds(0, count - 1)]
        pltpu.make_async_copy(part, part, sem).wait()

    barrier = pltpu.get_barrier_semaphore()
    peers(
        lambda to: pl.semaphore_signal(
            barrier, inc=1, device_id={"blk": to}, device_id_type=MESH
        )
    )

    for c in range(slots):
        fetch(c, c).start()

    place = lax.broadcasted_iota(jnp.int32, (anchor_rows, LANES), 0) * LANES
    place = place + lax.broadcasted_iota(jnp.int32, (anchor_rows, LANES), 1)
    mine = jnp.zeros((anchor_rows, LANES), jnp.int32)
    for w in range(wd):
        mine = jnp.where(place == slot_ref[w], me * wd + w, mine)
    contrib[...] = mine

    pack = LANES // occ
    deep = occ // pack
    flat = iv_ref[...].astype(jnp.float32)
    for t in range(deep):
        ivf[pl.ds(t, wd, stride=deep), :] = flat[:, t * LANES:(t + 1) * LANES]
    lane = lax.broadcasted_iota(jnp.int32, (deep, LANES), 1)
    for w in range(wd):
        v = ivf[w * deep:(w + 1) * deep, :]
        for e in range(pack):
            kept = jnp.where(lane // occ == e, v, 0.0)
            for h in range(pack):
                turned = kept if h == e else pltpu.roll(kept, (h - e) * occ % LANES, 1)
                bdf[pl.ds(w * LANES + h * occ + e, deep, stride=pack), :] = turned

    group = min(n, 16)
    bd = [bdf[w * LANES:(w + 1) * LANES, :].astype(jnp.bfloat16) for w in range(wd)]

    def make(g, carry):
        at = pl.multiple_of(g * group * rows, group * rows)
        for w in range(wd):
            x = lax.dot_general(
                wk_ref[w, pl.ds(at, group * rows), :], bd[w],
                (((1,), (1,)), ((), ())), preferred_element_type=jnp.float32,
            ).astype(jnp.bfloat16)
            for d in range(group):
                gsend[g * group + d, w * rows:(w + 1) * rows, :] = x[d * rows:(d + 1) * rows]
        return carry

    lax.fori_loop(0, n // group, make, 0)

    pl.semaphore_wait(barrier, n - 1)
    push(lambda to: contrib, arecv.at[me], 0)
    push(lambda to: gsend.at[to], grecv.at[me], 1)

    def lay(d, carry):
        at = pl.multiple_of(d * rows, rows)
        for w in range(wd):
            wsend[d, w * rows:(w + 1) * rows, :] = wk_ref[w, pl.ds(at, rows), :]
        row = lax.broadcasted_iota(jnp.int32, (tail, LANES), 0)
        share = jnp.zeros((tail, LANES), jnp.float32)
        for w in range(wd):
            for p in range(max(1, deep // n)):
                line = ivf[pl.ds(w * deep + d * deep // n + p, 1), :]
                share = jnp.where(row == w * (tail // wd) + p, line, share)
        wsend[d, blk:blk + tail, :] = share.astype(jnp.bfloat16)
        return carry

    lax.fori_loop(0, n, lay, 0)
    arecv[me] = mine
    grecv[me] = gsend[me]
    wrecv[me] = wsend[me]

    drain(arecv, recv_sem.at[0], n)

    def add(d, total):
        return total + arecv[d]

    anchor_v[...] = lax.fori_loop(0, n, add, jnp.zeros((anchor_rows, LANES), jnp.int32))
    to_scalar = pltpu.make_async_copy(anchor_v, anchor_s, local_sem)
    to_scalar.start()
    to_scalar.wait()

    drain(grecv, recv_sem.at[1], n)

    def source(s):
        return jnp.clip(anchor_s[s // LANES, s % LANES] // wd, 0, n - 1)

    def permute(d, carry):
        for w in range(wd):
            s = d * wd + w
            at = (lax.rem(d, 2) * chips + d // 2) * wd + w
            at = pl.multiple_of(at * rows, rows)
            gflat[pl.ds(at, rows), :] = grecv[
                source(s), w * rows:(w + 1) * rows, :
            ].astype(jnp.float32)
        return carry

    lax.fori_loop(0, n, permute, 0)
    for r in range(green.shape[1] // LANES):
        green[:, r * LANES:(r + 1) * LANES] = gflat[
            pl.ds(r, wt, stride=rows), :
        ].astype(jnp.bfloat16)

    def move(d, carry):
        for w in range(wd):
            msend[d, w * rows:(w + 1) * rows, :] = wrecv[
                source(d * wd + w), w * rows:(w + 1) * rows, :
            ]
        row = lax.broadcasted_iota(jnp.int32, (tail, LANES), 0)
        piece = jnp.zeros((tail, LANES), jnp.float32)
        for w in range(wd):
            got = wrecv[source(d * wd + w), blk:blk + tail, :].astype(jnp.float32)
            piece = jnp.where(row // (tail // wd) == w, got, piece)
        msend[d, blk:blk + tail, :] = piece.astype(jnp.bfloat16)
        return carry

    def swap(b):
        at = pl.multiple_of((1 - core) * half, half)
        return pltpu.make_async_remote_copy(
            src_ref=ftmp.at[b, pl.ds(at, half)], dst_ref=xrecv.at[b],
            send_sem=send_sem.at[4 + batches + b], recv_sem=recv_sem.at[4 + batches + b],
            device_id={"blk": chip * 2 + 1 - core}, device_id_type=MESH,
        )

    def combine(b):
        swap(b).wait_recv()

        def pair(p):
            mine = pl.multiple_of(core * half + p * size, size)
            other = pl.multiple_of(p * size, size)
            return ftmp[b, pl.ds(mine, size), :] + xrecv[b, pl.ds(other, size), :]

        def cast(p, carry):
            fsend[b, p] = pair(p).astype(jnp.bfloat16)
            return carry

        lax.fori_loop(0, chips, cast, 0)
        own[b] = pair(chip)

        def one(i, carry):
            p = lax.rem(chip + i, chips)
            pltpu.make_async_remote_copy(
                src_ref=fsend.at[b, p], dst_ref=frecv.at[b, chip],
                send_sem=send_sem.at[4 + b], recv_sem=recv_sem.at[4 + b],
                device_id={"blk": p * 2 + core}, device_id_type=MESH,
            ).start()
            return carry

        lax.fori_loop(1, chips, one, 0)

    def step(c, carry):
        k = lax.rem(c, slots)
        b = c // per_batch
        q = lax.rem(c, per_batch)
        fetch(c, k).wait()
        acc = jnp.dot(green[...], ring[k], preferred_element_type=jnp.float32)

        @pl.when(c + slots < chunks)
        def _():
            fetch(c + slots, k).start()

        for j in range(tiles):
            ftmp[b, pl.ds(q * tiles + j, wt, stride=span), :] = acc[:, j * LANES:(j + 1) * LANES]

        @pl.when(c == 0)
        def _():
            push(lambda to: wsend.at[to], wrecv.at[me], 2)

        @pl.when(c == min(chunks - 1, 6))
        def _():
            drain(wrecv, recv_sem.at[2], n)
            lax.fori_loop(0, n, move, 0)
            push(lambda to: msend.at[to], mrecv.at[me], 3)
            mrecv[me] = msend[me]

        @pl.when((q == 1) & (b > 0))
        def _():
            combine(b - 1)

        @pl.when(q == per_batch - 1)
        def _():
            swap(b).start()

        return carry

    lax.fori_loop(0, chunks, step, 0)
    combine(batches - 1)

    drain(mrecv, recv_sem.at[3], n)

    def keep(d, carry):
        at = pl.multiple_of(d * rows, rows)
        for w in range(wd):
            walk_ref[w, pl.ds(at, rows), :] = mrecv[d, w * rows:(w + 1) * rows, :]
        piece_ref[d] = mrecv[d, blk:blk + tail, :]
        return carry

    lax.fori_loop(0, n, keep, 0)

    def finish(b, carry):
        drain(frecv.at[b], recv_sem.at[4 + b], chips)

        def plus(i, total):
            return total + frecv[b, lax.rem(chip + i, chips)].astype(jnp.float32)

        total = lax.fori_loop(1, chips, plus, own[b])
        at = pl.multiple_of(b * span, span)
        for w in range(wd):
            force_ref[w, pl.ds(at, span), :] = total[w * span:(w + 1) * span]
        return carry

    lax.fori_loop(0, batches, finish, 0)
    drain(arecv, send_sem.at[0], n)
    drain(gsend, send_sem.at[1], n)
    drain(wsend, send_sem.at[2], n)
    drain(msend, send_sem.at[3], n)

    def sent(b, carry):
        drain(fsend.at[b], send_sem.at[4 + b], chips)
        swap(b).wait_send()
        return carry

    lax.fori_loop(0, batches, sent, 0)


def local(walkers, intersection_inv, new_slot, cholesky):
    n = lax.axis_size("blk")
    wd = walkers.shape[0]
    wt = n * wd
    orbitals, occ, ncol = cholesky.shape
    depth = orbitals * occ
    real = depth // LANES
    rows = -(-real // 16) * 16
    chol = cholesky.reshape(depth, ncol)

    wk = walkers.reshape(wd, n * real, LANES)
    if rows != real:
        wk = jnp.pad(
            wk.reshape(wd, n, real, LANES), ((0, 0), (0, 0), (0, rows - real), (0, 0))
        ).reshape(wd, n * rows, LANES)
    deep = occ * occ // LANES
    part = max(16 // wd, -(-deep // n))
    tail = wd * part
    anchor_rows = 8 * -(-wt // (8 * LANES))

    cols = 512
    per_batch = 4 if ncol % 2048 == 0 else 2
    chunks = ncol // cols
    batches = chunks // per_batch
    span = per_batch * cols // LANES
    bf, f32 = jnp.bfloat16, jnp.float32
    blk = wd * rows
    bufs = [
        ((n, blk, LANES), bf),
        ((n, blk, LANES), bf),
        ((n, blk + tail, LANES), bf),
        ((n, blk + tail, LANES), bf),
        ((n, blk + tail, LANES), bf),
        ((n, blk + tail, LANES), bf),
        ((anchor_rows, LANES), jnp.int32),
        ((n, anchor_rows, LANES), jnp.int32),
        ((anchor_rows, LANES), jnp.int32),
    ]
    more = [
        ((wd * deep, LANES), f32),
        ((wd * LANES, LANES), f32),
        ((wt * rows, LANES), f32),
        ((wt, depth), bf),
        ((batches, wt * span, LANES), f32),
        ((batches, wt * span // 2, LANES), f32),
        ((batches, n // 2, wd * span, LANES), bf),
        ((batches, n // 2, wd * span, LANES), bf),
        ((batches, wd * span, LANES), f32),
    ]

    def size(shape, dtype):
        total = jnp.dtype(dtype).itemsize
        for d in shape:
            total *= d
        return total

    used = sum(size(*b) for b in bufs + more)
    used += 2 * size((n, blk + tail, LANES), bf) + size((wd, ncol), f32)
    slots = min(chunks, (56 * MIB - used) // size((depth, cols), bf))

    vmem = pl.BlockSpec(memory_space=pltpu.VMEM)
    walk, piece, force = pl.pallas_call(
        functools.partial(
            kernel, n, wd, occ, rows, tail, batches, per_batch, slots, anchor_rows
        ),
        out_shape=(
            jax.ShapeDtypeStruct((wd, n * rows, LANES), bf),
            jax.ShapeDtypeStruct((n, tail, LANES), bf),
            jax.ShapeDtypeStruct((wd, ncol // LANES, LANES), f32),
        ),
        in_specs=[
            vmem, vmem,
            pl.BlockSpec(memory_space=pltpu.SMEM),
            pl.BlockSpec(memory_space=pl.ANY),
        ],
        out_specs=(vmem, vmem, vmem),
        scratch_shapes=[
            pltpu.VMEM((slots, depth, cols), bf),
            *[pltpu.VMEM(*b) for b in bufs],
            pltpu.SMEM((anchor_rows, LANES), jnp.int32),
            *[pltpu.VMEM(*b) for b in more],
            pltpu.SemaphoreType.DMA((slots,)),
            pltpu.SemaphoreType.DMA,
            pltpu.SemaphoreType.DMA((4 + 2 * batches,)),
            pltpu.SemaphoreType.DMA((4 + 2 * batches,)),
        ],
        compiler_params=pltpu.CompilerParams(
            collective_id=0, has_side_effects=True, vmem_limit_bytes=60 * MIB
        ),
        cost_estimate=pl.CostEstimate(
            flops=2 * wt * depth * ncol, bytes_accessed=2 * depth * ncol, transcendentals=0
        ),
    )(wk, intersection_inv, new_slot, chol)

    if rows != real:
        walk = walk.reshape(wd, n, rows, LANES)[:, :, :real]
    moved_walk = walk.reshape(wd, n * depth)
    took = max(1, deep // n)
    moved_inverse = (
        piece.reshape(n, wd, part, LANES)[::max(1, n // deep), :, :took]
        .transpose(1, 0, 2, 3).reshape(wd, occ * occ)
    )
    force_bias = force.reshape(wd, ncol)
    return (moved_walk, moved_inverse, force_bias)


def solution(mesh):
    placed = (
        P(("groups", "blk"), None),
        P(("groups", "blk"), None),
        P(("groups", "blk")),
        P(("groups", "blk"), None, None),
    )
    return jax.shard_map(
        local,
        mesh=mesh,
        in_specs=placed,
        out_specs=(
            P(("groups", "blk"), None),
            P(("groups", "blk"), None),
            P(("groups", "blk"), None),
        ),
        check_vma=False,
    )
```

time: 62.4 us -> 54 us (0.87)
  local copies, waits for them, and re-layouts: 10.8 us -> 6.66 us
  other arithmetic: 2.6 us -> 0 us
  Pallas kernels: 48 us -> 46.4 us
    slice x4 -> x0, local copies, waits for them, and re-layouts: 3.75 us -> none  [the longest x2 1.47 us: local(): moved[:, blk:].reshape(n, wd, part * LANES)[:, :, :share].transpose(1, 0, 2)]
    select_n x1 -> x0, other arithmetic: 1.96 us -> none  [local(): contrib = jnp.where(place == new_slot[w], me * wd + w, contrib)]
    unnamed x3, local copies, waits for them, and re-layouts: 3.36 us -> 5.17 us
    pallas_call x1, Pallas kernels: 48 us -> 46.4 us  [local(): pl.pallas_call(functools.partial(kernel, n, wd, occ, rows, tail, batches,...]
    mul x5 -> x0, local copies, waits for them, and re-layouts: 1.19 us -> none  [local(): eye[None, :, None, :, None] * inv[:, None, :, None, :]]
    reshape x4 -> x1, local copies, waits for them, and re-layouts: 1.68 us -> 0.62 us  [local(): moved_inverse = piece.reshape(n, wd, part, LANES)[::max(1, n // deep), :,...]
    transpose x1 -> x2, local copies, waits for them, and re-layouts: 0.02 us -> 0.86 us  [local(): moved_inverse = piece.reshape(n, wd, part, LANES)[::max(1, n // deep), :,...]
    pad x1 -> x0, local copies, waits for them, and re-layouts: 0.76 us -> none  [local(): jnp.pad(intersection_inv.reshape(wd, n, share).transpose(1, 0, 2), ((0, 0...]
where the time goes in v2:
time: 54 us; the launch traced here: 53.7 us
  Pallas kernels  46.4 us (86%)
  local copies, waits for them, and re-layouts  6.66 us (12%)
  between operations  0.65 us (1%)
    pallas_call x1, Pallas kernels, local(): pl.pallas_call(functools.partial(kernel, n, wd, occ, rows, tail, batches,...  46.4 us
    unnamed x3, local copies, waits for them, and re-layouts  5.17 us

profile of v2, /device:TPU:0, one launch (start us, length us, event | category | flops | bytes accessed | tf_op | source)
XLA Modules:
  0.0 53.7 jit_solution(6581893178365688040)
XLA Ops:
  0.6 1.7 %copy.15 = bf16[1,2,512,128]{3,2,1,0:T(8,128)(2,1)} copy(bf16[1,2,512,128]{3,1,2,0:T(2,128)(2,1)} %bitcast.17) | data formatting | bytes 524288
  2.3 46.4 %shard_map.67 = (bf16[2,512,128]{2,1,0:T(8,128)(2,1)}, bf16[16,16,128]{2,1,0:T(8,128)(2,1)}, f32[2,80,128]{2,1,0:T(8,128)}) custom-call(bf16[2,512,128]{2,1,0:T(8,128)(2,1)} %bitcast.16, bf16[2,4096]{1,0:T(2,128)(2,1)} %iv_ref.1, s32[2]{0:T(128)} %slot_ref.1, bf16[4096,10240]{1,0:T(8,128)(2,1)} %bitcast.chol_ref), custom_call_target="tpu_custom_call" | custom-call | flops 2684354560 | bytes 83886080 | tf_op jit(solution)/shard_map/pallas_call | solution.py:346
  48.7 1.9 %copy.14 = bf16[1,2,512,128]{3,1,2,0:T(2,128)(2,1)} copy(bf16[1,2,512,128]{3,2,1,0:T(8,128)(2,1)} %bitcast.19) | data formatting | bytes 524288
  50.6 0.8 %slice_bitcast_fusion = bf16[2,16,2,128]{3,2,0,1:T(2,128)(2,1)S(1)} fusion(bf16[16,2,8,128]{3,2,1,0:T(8,128)(2,1)} %bitcast.22), kind=kLoop, calls=%fused_computation.3 | loop fusion | bytes 32768 | tf_op jit(solution)/shard_map/transpose | solution.py:385
  51.5 0.6 %reshape.28 = bf16[2,4096]{1,0:T(2,128)(2,1)} reshape(bf16[2,16,2,128]{3,2,1,0:T(2,128)(2,1)S(1)} %copy.7) | data formatting | bytes 32768 | tf_op jit(solution)/shard_map/reshape | solution.py:385
  52.1 1.6 %copy.16 = f32[1,2,80,128]{3,1,2,0:T(2,128)} copy(f32[1,2,80,128]{3,2,1,0:T(8,128)} %bitcast.20) | data formatting | bytes 163840
  (1 shorter events, 0.0 us)
